TPU v7x, 512 devices: a whole 4x8x8 slice. The times are simulated.
512 devices in a mesh: ctx: 64 (over z_lo, y, core), head: 8 (over z_hi, x).
Axes of the slice: x: 4, y: 8, z: 8 (z_hi: 2, z_lo: 4; z = z_hi * 4 + z_lo), core: 2. Of those that a mesh axis runs over, the one named last changes fastest.
Arguments:
- queries: bfloat16 [8192, 4096], P('ctx', 'head'), may hold values from -4.5 to 4.5
- key_states: bfloat16 [8192, 4096], P('ctx', 'head'), may hold values from -4.5 to 4.5
- values: bfloat16 [8192, 4096], P('ctx', 'head'), may hold values from -6 to 6
- out_grad: bfloat16 [8192, 4096], P(('ctx', 'head')), may hold values from -6 to 6
- pattern: int32 [64, 3], replicated, may hold values from 0 to 63, as said below
- global_ids: int32 [2], replicated, may hold values from 0 to 63, as said below
Outputs:
- query_grad: bfloat16 [8192, 4096], P('ctx', 'head')
- key_grad: bfloat16 [8192, 4096], P('ctx', 'head')
- value_grad: bfloat16 [8192, 4096], P('ctx', 'head')
Inputs may be any that keep to these rules, and one draw needn't show every extreme that they name: Each pattern[b, r] is a block of the context shard of query block b or of one of the two shards beside it on the circular sequence: pattern[b, r] - b is -1, 0 or 1 modulo 64. `global_ids`: 2 different blocks; the last entry is the sequence's last block, 63.
All inputs are finite; a program needn't handle non-finite values.
Results may differ from a plain program's by a relative error of at most 0.009.
Values may be sent and summed in bfloat16 or wider, within the bound.
A program may use at most 64 MiB of HBM per device.

v0:
```python
import math

import jax
import jax.numpy as jnp
from jax import lax
from jax.sharding import PartitionSpec as P

HD = 128
BLK = 128
GLB = 2


def padded(cells, sides, width):
    for axis, dim in sides:
        count = lax.axis_size(axis)
        head = lax.slice_in_dim(cells, 0, width, axis=dim)
        tail = lax.slice_in_dim(cells, cells.shape[dim] - width, cells.shape[dim], axis=dim)
        cells = jnp.concatenate(
            [
                lax.ppermute(tail, axis, [(i, (i + 1) % count) for i in range(count)]),
                cells,
                lax.ppermute(head, axis, [((i + 1) % count, i) for i in range(count)]),
            ],
            axis=dim,
        )
    return cells


def from_root(value, axis, root):
    mine = lax.axis_index(axis) == root
    return lax.psum(jnp.where(mine, value, jnp.zeros_like(value)), axis)


def window_slot(block_ids, cycle_place, cycle_size, per_shard):
    owner_shard = block_ids // per_shard
    offset = (owner_shard - cycle_place) % cycle_size
    which_side = jnp.where(offset == 0, 1, jnp.where(offset == 1, 2, 0))
    return which_side * per_shard + block_ids % per_shard


def near_lists(block_ids, pattern, block_total):
    local_ids = jnp.stack(
        [(block_ids - 1) % block_total, block_ids, (block_ids + 1) % block_total], axis=1
    )
    return jnp.concatenate([local_ids, pattern[block_ids]], axis=1)


def block_pass(query_blk, grad_blk, kv_ent, slot_row, store_count):
    feat_width = query_blk.shape[-1]
    head_count = feat_width // HD
    entry_count = kv_ent.shape[0]
    score_scale = 1.0 / math.sqrt(HD)
    query_heads = query_blk.reshape(BLK, head_count, HD)
    grad_heads = grad_blk.reshape(BLK, head_count, HD)
    key_heads = kv_ent[:, :, :feat_width].reshape(entry_count, BLK, head_count, HD)
    value_heads = kv_ent[:, :, feat_width:].reshape(entry_count, BLK, head_count, HD)
    scores = (
        jnp.einsum("ihd,ejhd->hiej", query_heads, key_heads, preferred_element_type=jnp.float32)
        * score_scale
    )
    dprobs = jnp.einsum(
        "ihd,ejhd->hiej", grad_heads, value_heads, preferred_element_type=jnp.float32
    )
    row_top = jnp.max(scores, axis=(2, 3), keepdims=True)
    log_total = row_top + jnp.log(jnp.sum(jnp.exp(scores - row_top), axis=(2, 3), keepdims=True))
    prob_full = jnp.exp(scores - log_total)
    deltas = jnp.sum(prob_full * dprobs, axis=(2, 3), keepdims=True)
    score_grad = (prob_full * (dprobs - deltas) * score_scale).astype(jnp.bfloat16)
    prob_low = prob_full.astype(jnp.bfloat16)
    query_part = jnp.einsum(
        "hiej,ejhd->ihd", score_grad, key_heads, preferred_element_type=jnp.float32
    )
    key_part = jnp.einsum(
        "hiej,ihd->ejhd", score_grad, query_heads, preferred_element_type=jnp.float32
    )
    value_part = jnp.einsum(
        "hiej,ihd->ejhd", prob_low, grad_heads, preferred_element_type=jnp.float32
    )
    both_grads = jnp.concatenate(
        [
            key_part.reshape(entry_count, BLK, feat_width),
            value_part.reshape(entry_count, BLK, feat_width),
        ],
        axis=2,
    )
    spare_store = jnp.zeros((store_count + 1, BLK, 2 * feat_width), jnp.float32)
    safe_slots = jnp.minimum(slot_row, store_count)
    store_part = spare_store.at[safe_slots].add(both_grads)[:store_count]
    return (query_part.reshape(BLK, feat_width), store_part, log_total, deltas)


def shards(queries, key_states, values, out_grad, pattern, global_ids):
    tok_rows, feat_width = queries.shape
    head_count = feat_width // HD
    per_shard = tok_rows // BLK
    cycle_size = lax.axis_size("ctx")
    cycle_place = lax.axis_index("ctx")
    block_total = per_shard * cycle_size
    grad_rows = lax.all_to_all(out_grad, "head", split_axis=1, concat_axis=0, tiled=True)
    kv_pair = jnp.concatenate([key_states, values], axis=1)
    own_store = kv_pair.reshape(per_shard, BLK, 2 * feat_width)
    window = padded(kv_pair, (("ctx", 0),), tok_rows)
    gl_owner = global_ids // per_shard
    gl_local = global_ids % per_shard
    pieces = []
    for gl_index in range(GLB):
        pieces.append(from_root(own_store[gl_local[gl_index]], "ctx", gl_owner[gl_index]))
    global_kv = jnp.stack(pieces)
    key_store = jnp.concatenate(
        [window.reshape(3 * per_shard, BLK, 2 * feat_width), global_kv], axis=0
    )
    store_count = 3 * per_shard + GLB
    own_ids = cycle_place * per_shard + jnp.arange(per_shard, dtype=jnp.int32)
    own_lists = near_lists(own_ids, pattern, block_total)
    global_slots = 3 * per_shard + jnp.arange(GLB, dtype=jnp.int32)[None, :]
    own_slots = jnp.concatenate(
        [window_slot(own_lists, cycle_place, cycle_size, per_shard), global_slots], axis=1
    )
    query_blocks = queries.reshape(per_shard, BLK, feat_width)
    grad_blocks = grad_rows.reshape(per_shard, BLK, feat_width)

    def own_step(block_num, state_now):
        query_all, store_sum, total_all, delta_all = state_now
        slot_row = own_slots[block_num]
        results = block_pass(
            query_blocks[block_num],
            grad_blocks[block_num],
            key_store[slot_row],
            slot_row,
            store_count,
        )
        query_all = query_all.at[block_num].set(results[0])
        total_all = total_all.at[block_num].set(results[2][:, :, 0, 0])
        delta_all = delta_all.at[block_num].set(results[3][:, :, 0, 0])
        return (query_all, store_sum + results[1], total_all, delta_all)

    initial = (
        jnp.zeros((per_shard, BLK, feat_width), jnp.float32),
        jnp.zeros((store_count, BLK, 2 * feat_width), jnp.float32),
        jnp.zeros((per_shard, head_count, BLK), jnp.float32),
        jnp.zeros((per_shard, head_count, BLK), jnp.float32),
    )
    query_all, store_sum, total_all, delta_all = lax.fori_loop(0, per_shard, own_step, initial)
    global_sum = lax.psum(store_sum[3 * per_shard :], "ctx")
    own_sum = store_sum[per_shard : 2 * per_shard]
    sendback = jnp.concatenate(
        [store_sum[:per_shard], store_sum[2 * per_shard : 3 * per_shard]], axis=0
    ).reshape(2 * tok_rows, 2 * feat_width)
    beside_all = padded(sendback.astype(jnp.bfloat16), (("ctx", 0),), tok_rows).astype(
        sendback.dtype
    )
    own_sum = own_sum + (beside_all[:tok_rows] + beside_all[3 * tok_rows :]).reshape(
        per_shard, BLK, 2 * feat_width
    )
    owner_pick = (
        (gl_owner[:, None] == cycle_place)
        & (gl_local[:, None] == jnp.arange(per_shard, dtype=jnp.int32)[None, :])
    ).astype(jnp.float32)
    own_sum = own_sum + jnp.einsum(
        "gl,gjf->ljf", owner_pick, global_sum, precision=lax.Precision.HIGHEST
    )
    query_grad = query_all.reshape(tok_rows, feat_width).astype(jnp.bfloat16)
    key_grad = own_sum[:, :, :feat_width].reshape(tok_rows, feat_width).astype(jnp.bfloat16)
    value_grad = own_sum[:, :, feat_width:].reshape(tok_rows, feat_width).astype(jnp.bfloat16)
    return (query_grad, key_grad, value_grad)


def solution(mesh):
    placed = (
        P("ctx", "head"),
        P("ctx", "head"),
        P("ctx", "head"),
        P(("ctx", "head"), None),
        P(),
        P(),
    )
    return jax.shard_map(
        shards,
        mesh=mesh,
        in_specs=placed,
        out_specs=(P("ctx", "head"), P("ctx", "head"), P("ctx", "head")),
        check_vma=False,
    )
```

profile of v0, /device:TPU:1, one launch (start us, length us, event | category | flops | bytes accessed | tf_op | source)
XLA Modules:
  0.0 1139.9 jit_solution(16863365047862252026)
XLA Ops:
  7.2 0.9 constant_dynamic-update-slice_fusion.1
  8.1 0.9 constant_dynamic-update-slice_fusion
  9.1 8.8 collective-permute-start.1
  17.9 1.9 collective-permute-start
  19.8 1.6 copy.84
  21.4 8.3 all-to-all-start
  29.7 1.4 fusion.29
  32.3 0.8 select_bitcast_fusion.1
  33.7 5.3 all-to-all-done
  39.9 529.8 %all-reduce.6.cloned.1.call-done = (bf16[1,128,1024]{2,1,0:T(8,128)(2,1)}, bf16[1,128,1024]{2,1,0:T(8,128)(2,1)}) async-done(((bf16[1,128,1024]{2,1,0:T(8,128)(2,1)}, bf16[1,128,1024]{2,1,0:T(8,128)(2,1)}), (bf16[1,128,1024]{2,1,0:T(8,128)(2,1)}, bf16[1,128,1024]{2,1,0:T(8,128)(2,1)})) %all-reduce.6.cloned.1.call-update) | async-done | bytes 524304 | tf_op jit(solution)/shard_map/psum | solution.py:31
  569.7 1.2 pad_maximum_fusion.1
  571.6 1.2 fusion.28
  578.7 2.3 pad_maximum_fusion
  580.9 5.4 copy.45
  586.7 5.8 scatter_fusion
  592.6 1.1 slice.113
  593.7 1.4 convert.10
  597.0 2.0 slice_bitcast_fusion.3
  598.9 2.9 collective-permute-start.2
  601.9 2.1 collective-permute-start.3
  604.0 0.8 pad_maximum_fusion.3
  604.8 522.5 %all-reduce.4.cloned.1.call-done = f32[2,128,1024]{2,1,0:T(8,128)} async-done(((f32[2,128,1024]{2,1,0:T(8,128)}), f32[2,128,1024]{2,1,0:T(8,128)}) %all-reduce.4.cloned.1.call-update) | async-done | bytes 1048592 | tf_op jit(solution)/shard_map/psum | solution.py:144
  1127.3 3.8 fusion.17
  1131.1 1.2 fusion.22
  (55 shorter events, 10.9 us)
Async XLA Ops:
  7.2 26.1 %copy-start = (s32[64,3]{0,1:T(4,128)S(1)}, s32[64,3]{0,1:T(4,128)}, u32[]{:S(2)}) copy-start(s32[64,3]{0,1:T(4,128)} %param.12) | copy-start | bytes 2308
  7.2 26.2 %copy-start.8 = (bf16[128,512]{1,0:T(8,128)(2,1)S(1)}, bf16[128,512]{1,0:T(8,128)(2,1)}, u32[]{:S(2)}) copy-start(bf16[128,512]{1,0:T(8,128)(2,1)} %param.8) | copy-start | bytes 393220
  9.1 30.8 %collective-permute-start.1 = (bf16[128,1024]{1,0:T(8,128)(2,1)S(1)}, bf16[128,1024]{1,0:T(8,128)(2,1)S(1)}, u32[]{:S(2)}, u32[]{:S(2)}) collective-permute-start(bf16[128,1024]{1,0:T(8,128)(2,1)S(1)} %constant_dynamic-update-slice_fusion), channel_id=1, source_target_pairs={{8,0},{16,8},{24,16},{32,24},{40,32},{48,40},{56,48},{64,56},{72,6... | collective-permute-start | bytes 786440 | tf_op jit(solution)/shard_map/ppermute | solution.py:22
  17.9 22.0 %collective-permute-start = (bf16[128,1024]{1,0:T(8,128)(2,1)S(1)}, bf16[128,1024]{1,0:T(8,128)(2,1)S(1)}, u32[]{:S(2)}, u32[]{:S(2)}) collective-permute-start(bf16[128,1024]{1,0:T(8,128)(2,1)S(1)} %constant_dynamic-update-slice_fusion), channel_id=1, source_target_pairs={{0,8},{8,16},{16,24},{24,32},{32,40},{40,48},{48,56},{56,64},{64,7... | collective-permute-start | bytes 786440 | tf_op jit(solution)/shard_map/ppermute | solution.py:20
  21.4 17.7 %all-to-all-start = ((bf16[16,8,512]{2,0,1:T(8,128)(2,1)}), bf16[16,8,512]{2,0,1:T(8,128)(2,1)S(1)}, u32[]{:S(2)}, u32[]{:S(2)}) async-start(bf16[16,8,512]{2,0,1:T(8,128)(2,1)} %bitcast.99), calls=%async_computation | async-start | bytes 262144 | tf_op jit(solution)/shard_map/all_to_all | solution.py:99
  29.6 540.1 %all-reduce.6.cloned.1.call-start = ((), (), s32[]{:S(2)}) async-start(), calls=%async_computation.2 | async-start | bytes 1048576 | tf_op jit(solution)/shard_map/psum | solution.py:31
  33.2 1094.1 %all-reduce.4.cloned.1.call-start = ((), (), s32[]{:S(2)}) async-start(), calls=%async_computation.1 | async-start | bytes 2097152 | tf_op jit(solution)/shard_map/psum | solution.py:144
  572.8 1.2 copy-start.5
  574.7 1.1 copy-start.3
  574.7 1.1 copy-start.7
  577.7 1.0 copy-start.1
  593.6 1.4 copy-start.2
  593.7 2.1 copy-start.4
  595.8 531.5 %copy-start.9 = (s32[2]{0:T(128)S(1)}, s32[2]{0:T(128)}, u32[]{:S(2)}) copy-start(s32[2]{0:T(128)} %param.13) | copy-start | bytes 28
  598.9 532.2 %collective-permute-start.2 = (bf16[128,1024]{1,0:T(8,128)(2,1)}, bf16[128,1024]{1,0:T(8,128)(2,1)S(1)}, u32[]{:S(2)}, u32[]{:S(2)}) collective-permute-start(bf16[128,1024]{1,0:T(8,128)(2,1)} %get-tuple-element.68), channel_id=1, source_target_pairs={{0,8},{8,16},{16,24},{24,32},{32,40},{40,48},{48,56},{56,64},{64,7... | collective-permute-start | bytes 786440 | tf_op jit(solution)/shard_map/ppermute | solution.py:20
  601.9 529.2 %collective-permute-start.3 = (bf16[128,1024]{1,0:T(8,128)(2,1)}, bf16[128,1024]{1,0:T(8,128)(2,1)}, u32[]{:S(2)}, u32[]{:S(2)}) collective-permute-start(bf16[128,1024]{1,0:T(8,128)(2,1)} %get-tuple-element.69), channel_id=1, source_target_pairs={{8,0},{16,8},{24,16},{32,24},{40,32},{48,40},{56,48},{64,56},{72,6... | collective-permute-start | bytes 786440 | tf_op jit(solution)/shard_map/ppermute | solution.py:22
  1127.3 3.8 copy-start.6
Sparse Core Ops, SparseCore 0:
  33.4 536.2 all-reduce.5
  593.8 533.4 all-reduce.3
where the time goes:
time: 1140 us
  waiting for transfers between devices  1060 us (93%)
  starting transfers between devices  24.1 us (2%)
  local copies, waits for them, and re-layouts  21.4 us (2%)
  between operations  15.6 us (1%)
  other arithmetic  14.7 us (1%)
    psum x1, waiting for transfers between devices, from_root(): return lax.psum(jnp.where(mine, value, jnp.zeros_like(value)), axis)  530 us
    psum x1, waiting for transfers between devices, shards(): global_sum = lax.psum(store_sum[3 * per_shard:], 'ctx')  522 us
  transfers between devices with their start and end apart: 7, of which 3 were waited for; matrix products, arithmetic and copies ran while one was open for 1% of the time, Pallas kernels for 0%

commit v1 on v0

v1 whole, which is shorter than its diff:
```python
import functools
import math

import jax
import jax.numpy as jnp
from jax import lax
from jax.experimental import pallas as pl
from jax.experimental.pallas import tpu as pltpu
from jax.sharding import PartitionSpec as P

HD = 128
BLK = 128
SCALE = 1.0 / math.sqrt(HD)
MESH = pl.DeviceIdType.MESH
BF = jnp.bfloat16
F32 = jnp.float32
NT = (((1,), (1,)), ((), ()))
NN = (((1,), (0,)), ((), ()))
TN = (((0,), (0,)), ((), ()))


def dot(a, b, dims):
    return lax.dot_general(a, b, dims, preferred_element_type=F32)


def kernel(
    pat, gid, q_ref, k_ref, v_ref, g_ref, dq_ref, dk_ref, dv_ref,
    q2, kv2, kvn, do2, cand, rsel, hold, gkv, gpart, rgr, hsum, gs0, gs63,
    nbo, nbi, own, fin, dqb, el, dpl, dsg,
    in_sem, pair_s, pair_r, nb_s, nb_r, do_s, do_r, sel_s, sel_r, sc_s, sc_r,
    ag_s, ag_r, rg_s, rg_r, gs_s, gs_r, gn_s, gn_r, out_l, out_s, out_r,
):
    me = lax.axis_index("ctx")
    head = lax.axis_index("head")
    core = me % 2
    chip = me // 2
    y = chip % 8
    z = chip // 8
    sib = {"ctx": chip * 2 + 1 - core}
    left = {"ctx": (me + 62) % 64}
    right = {"ctx": (me + 2) % 64}
    mine = pl.multiple_of(core * 256, 256)
    theirs = pl.multiple_of((1 - core) * 256, 256)

    def remote(src, dst, ss, rs, dev):
        return pltpu.make_async_remote_copy(
            src_ref=src, dst_ref=dst, send_sem=ss, recv_sem=rs,
            device_id=dev, device_id_type=MESH,
        )

    def local(src, dst, sem):
        return pltpu.make_async_copy(src, dst, sem)

    def wait(ref, sem):
        pltpu.make_async_copy(ref, ref, sem).wait()

    def far_y(i):
        return (y + 4 + (1 - 2 * (i % 2)) * ((i + 1) // 2)) % 8

    def plane(t):
        ty = far_y(t // 4)
        tz = (z + 3 - t % 4) % 4
        return ty, tz, {"ctx": (tz * 8 + ty) * 2 + core}

    def group(t):
        th = (head + 7 - t // 2) % 8
        tc = (core + 1 - t % 2) % 2
        return th, tc, {"ctx": chip * 2 + tc, "head": th}

    loads = [
        local(k_ref.at[:, pl.ds(mine, 256)], kv2.at[core, :, pl.ds(0, 256)], in_sem.at[0]),
        local(v_ref.at[:, pl.ds(mine, 256)], kv2.at[core, :, pl.ds(256, 256)], in_sem.at[1]),
        local(q_ref.at[:, pl.ds(mine, 256)], q2.at[core], in_sem.at[2]),
    ]
    for cp in loads:
        cp.start()

    bar = pltpu.get_barrier_semaphore()

    @pl.loop(0, 31)
    def _(t):
        pl.semaphore_signal(bar, inc=1, device_id=plane(t)[2], device_id_type=MESH)

    @pl.loop(0, 15)
    def _(t):
        pl.semaphore_signal(bar, inc=1, device_id=group(t)[2], device_id_type=MESH)

    pl.semaphore_wait(bar, 46)

    pairs = [
        remote(k_ref.at[:, pl.ds(theirs, 256)], kv2.at[core, :, pl.ds(0, 256)], pair_s.at[0], pair_r.at[0], sib),
        remote(v_ref.at[:, pl.ds(theirs, 256)], kv2.at[core, :, pl.ds(256, 256)], pair_s.at[1], pair_r.at[1], sib),
        remote(q_ref.at[:, pl.ds(theirs, 256)], q2.at[core], pair_s.at[2], pair_r.at[2], sib),
    ]
    for cp in pairs:
        cp.start()
    loads[0].wait()
    loads[1].wait()
    pairs[0].wait_recv()
    pairs[1].wait_recv()

    def piece(ref, tz, ty):
        return ref.at[pl.ds(pl.multiple_of(ty * 16, 16), 16), pl.ds(pl.multiple_of(tz * 128, 128), 128)]

    @pl.when(chip == 31)
    def _():
        @pl.loop(0, 31)
        def _(t):
            ty, tz, dev = plane(t)
            remote(piece(kv2.at[1], tz, ty), hold.at[1], sc_s, sc_r, dev).start()

        local(piece(kv2.at[1], z, y), hold.at[1], sc_r).start()

    g0 = gid[0]
    cand[...] = kv2[g0 % 2]

    @pl.loop(0, 31)
    def _(t):
        ty, tz, dev = plane(t)
        remote(piece(cand, tz, ty), rsel.at[chip], sel_s, sel_r, dev).start()

    local(piece(cand, z, y), rsel.at[chip], sel_r).start()

    nbk = [
        remote(kv2.at[1], kvn.at[0], nb_s.at[0], nb_r.at[0], right),
        remote(kv2.at[0], kvn.at[1], nb_s.at[1], nb_r.at[1], left),
    ]
    for cp in nbk:
        cp.start()

    rows = pl.ds(pl.multiple_of(head * 16, 16), 16)

    def gcols(th, tc):
        return pl.ds(pl.multiple_of(th * 512 + tc * 256, 256), 256)

    @pl.loop(0, 15)
    def _(t):
        th, tc, dev = group(t)
        remote(g_ref.at[:, gcols(th, tc)], do2.at[core, rows], do_s, do_r, dev).start()

    local(g_ref.at[:, gcols(head, core)], do2.at[core, rows], do_r).start()

    def spread(g):
        @pl.loop(0, 31)
        def _(t):
            _, _, dev = plane(t)
            remote(hold.at[g], piece(gkv.at[g], z, y), ag_s.at[g], ag_r.at[g], dev).start()

        local(hold.at[g], piece(gkv.at[g], z, y), ag_r.at[g]).start()

    wait(hold.at[1], sc_r)
    spread(1)
    wait(rsel, sel_r)
    hold[0] = rsel[g0 // 2]
    spread(0)

    loads[2].wait()
    pairs[2].wait_recv()
    nbk[0].wait_recv()
    nbk[1].wait_recv()
    wait(do2, do_r)

    def count(block, target):
        n = jnp.int32(1)
        for r in range(3):
            n = n + jnp.where(pat[block, r] == target, 1, 0)
        return n.astype(F32)

    b0, b1 = chip * 2, chip * 2 + 1
    bl, br = (b0 + 63) % 64, (b0 + 2) % 64
    lane = lax.broadcasted_iota(jnp.int32, (1, 256), 1) < 128
    mult = [
        jnp.where(lane, count(b0, bl), count(b1, br)),
        jnp.where(lane, count(b0, b0), count(b1, b0)),
        jnp.where(lane, count(b0, b1), count(b1, b1)),
    ]

    def cols(hh):
        return slice(hh * 128, hh * 128 + 128), slice(256 + hh * 128, 384 + hh * 128)

    stats = []
    for hh in range(2):
        kc, vc = cols(hh)
        qh = q2[:, :, kc].reshape(256, 128)
        gh = do2[:, :, kc].reshape(256, 128)
        s_out = jnp.concatenate([dot(kvn[0, :, kc], qh[:128], NT), dot(kvn[1, :, kc], qh[128:], NT)], axis=1) * SCALE
        s_in = dot(kv2[:, :, kc].reshape(256, 128), qh, NT) * SCALE
        top = jnp.maximum(jnp.max(s_out, axis=0, keepdims=True), jnp.max(s_in, axis=0, keepdims=True))
        e_out = jnp.exp(s_out - top) * mult[0]
        e_a = jnp.exp(s_in[:128] - top) * mult[1]
        e_b = jnp.exp(s_in[128:] - top) * mult[2]
        d_out = jnp.concatenate([dot(kvn[0, :, vc], gh[:128], NT), dot(kvn[1, :, vc], gh[128:], NT)], axis=1)
        d_in = dot(kv2[:, :, vc].reshape(256, 128), gh, NT)
        total = jnp.sum(e_out + e_a + e_b, axis=0, keepdims=True)
        dsum = jnp.sum(e_out * d_out + e_a * d_in[:128] + e_b * d_in[128:], axis=0, keepdims=True)
        el[hh, 0:128] = e_out
        el[hh, 128:256] = e_a
        el[hh, 256:384] = e_b
        dpl[hh, 0:128] = d_out
        dpl[hh, 128:384] = d_in
        stats.append((top, total, dsum))

    wait(gkv.at[1], ag_r.at[1])
    wait(gkv.at[0], ag_r.at[0])
    rowf = []
    for hh in range(2):
        kc, vc = cols(hh)
        top_l, total_l, dsum_l = stats[hh]
        qh = q2[:, :, kc].reshape(256, 128)
        gh = do2[:, :, kc].reshape(256, 128)
        s = dot(gkv[:, :, kc].reshape(256, 128), qh, NT) * SCALE
        dp = dot(gkv[:, :, vc].reshape(256, 128), gh, NT)
        top = jnp.maximum(top_l, jnp.max(s, axis=0, keepdims=True))
        e = jnp.exp(s - top)
        scale_l = jnp.exp(top_l - top)
        inv = 1.0 / (total_l * scale_l + jnp.sum(e, axis=0, keepdims=True))
        delta = (dsum_l * scale_l + jnp.sum(e * dp, axis=0, keepdims=True)) * inv
        p = e * inv
        ds = (p * (dp - delta) * SCALE).astype(BF)
        dsg[hh] = ds
        gpart[:, :, kc] = dot(ds, qh, NN).astype(BF).reshape(2, 128, 128)
        gpart[:, :, vc] = dot(p.astype(BF), gh, NN).astype(BF).reshape(2, 128, 128)
        rowf.append((scale_l * inv, delta))

        @pl.loop(0, 16)
        def _(t):
            ty = far_y(t // 2)
            tz = hh + 2 * (t % 2)
            src = gpart.at[:, pl.ds(pl.multiple_of(ty * 16, 16), 16), pl.ds(pl.multiple_of(tz * 128, 128), 128)]
            self_piece = jnp.logical_and(ty == y, tz == z)

            @pl.when(self_piece)
            def _():
                local(src, rgr.at[chip], rg_r).start()

            @pl.when(jnp.logical_not(self_piece))
            def _():
                remote(src, rgr.at[chip], rg_s, rg_r, {"ctx": (tz * 8 + ty) * 2 + core}).start()

    nbg = []
    for hh in range(2):
        kc, vc = cols(hh)
        qh = q2[:, :, kc].reshape(256, 128)
        gh = do2[:, :, kc].reshape(256, 128)
        rf, delta = rowf[hh]
        p0 = el[hh, 0:128] * rf
        ds0 = (p0 * (dpl[hh, 0:128] - delta) * SCALE).astype(BF)
        p0 = p0.astype(BF)
        nbo[0, hh, :, 0:128] = dot(ds0[:, :128], qh[:128], NN).astype(BF)
        nbo[0, hh, :, 128:256] = dot(p0[:, :128], gh[:128], NN).astype(BF)
        nbo[1, hh, :, 0:128] = dot(ds0[:, 128:], qh[128:], NN).astype(BF)
        nbo[1, hh, :, 128:256] = dot(p0[:, 128:], gh[128:], NN).astype(BF)
        for side, dev in ((0, left), (1, right)):
            cp = remote(nbo.at[side, hh], nbi.at[1 - side, hh], gn_s.at[side, hh], gn_r.at[1 - side, hh], dev)
            cp.start()
            nbg.append(cp)
        p1 = el[hh, 128:384] * rf
        ds1 = (p1 * (dpl[hh, 128:384] - delta) * SCALE).astype(BF)
        own[:, :, kc] = dot(ds1, qh, NN).reshape(2, 128, 128)
        own[:, :, vc] = dot(p1.astype(BF), gh, NN).reshape(2, 128, 128)
        dq = dot(ds1, kv2[:, :, kc].reshape(256, 128), TN)
        dq = dq + dot(dsg[hh], gkv[:, :, kc].reshape(256, 128), TN)
        dqb[0, :, kc] = (dq[:128] + dot(ds0[:, :128], kvn[0, :, kc], TN)).astype(BF)
        dqb[1, :, kc] = (dq[128:] + dot(ds0[:, 128:], kvn[1, :, kc], TN)).astype(BF)

    my_cols = pl.ds(mine, 256)
    outs = [
        remote(dqb.at[1 - core], dq_ref.at[:, my_cols], out_s.at[0], out_r.at[0], sib),
        local(dqb.at[core], dq_ref.at[:, my_cols], out_l.at[0]),
    ]
    for cp in outs:
        cp.start()

    wait(rgr, rg_r)
    acc = rgr[0].astype(F32)
    for j in range(1, 32):
        acc = acc + rgr[j].astype(F32)
    hsum[...] = acc.astype(BF)

    @pl.loop(0, 31)
    def _(t):
        _, _, dev = plane(t)
        remote(hsum.at[0], piece(gs0, z, y), gs_s.at[0], gs_r.at[0], dev).start()

    local(hsum.at[0], piece(gs0, z, y), gs_r.at[0]).start()

    @pl.when(chip == 31)
    def _():
        local(hsum.at[1], piece(gs63, z, y), gs_r.at[1]).start()

    @pl.when(chip != 31)
    def _():
        remote(hsum.at[1], piece(gs63, z, y), gs_s.at[1], gs_r.at[1], {"ctx": 62 + core}).start()

    for cp in nbg:
        cp.wait_recv()
    for b in range(2):
        for hh in range(2):
            kc, vc = cols(hh)
            own[b, :, kc] += nbi[b, hh, :, 0:128].astype(F32)
            own[b, :, vc] += nbi[b, hh, :, 128:256].astype(F32)

    @pl.when(chip == 31)
    def _():
        wait(gs63, gs_r.at[1])
        own[1] += gs63[...].astype(F32)

    wait(gs0, gs_r.at[0])
    for b in range(2):
        pick = jnp.where(g0 == b0 + b, 1.0, 0.0).astype(F32)
        fin[b] = (own[b] + gs0[...].astype(F32) * pick).astype(BF)

    lo, hi = pl.ds(0, 256), pl.ds(256, 256)
    more = [
        remote(fin.at[1 - core, :, lo], dk_ref.at[:, my_cols], out_s.at[1], out_r.at[1], sib),
        remote(fin.at[1 - core, :, hi], dv_ref.at[:, my_cols], out_s.at[2], out_r.at[2], sib),
        local(fin.at[core, :, lo], dk_ref.at[:, my_cols], out_l.at[1]),
        local(fin.at[core, :, hi], dv_ref.at[:, my_cols], out_l.at[2]),
    ]
    for cp in more:
        cp.start()

    for cp in pairs:
        cp.wait_send()
    for cp in nbk:
        cp.wait_send()
    for cp in nbg:
        cp.wait_send()

    @pl.when(chip == 31)
    def _():
        wait(rsel.at[pl.ds(0, 31)], sc_s)

    @pl.when(chip != 31)
    def _():
        wait(hsum.at[1], gs_s.at[1])

    wait(rsel.at[pl.ds(0, 31)], sel_s)
    wait(rsel.at[pl.ds(0, 30)], do_s)
    wait(rsel.at[pl.ds(0, 31)], ag_s.at[0])
    wait(rsel.at[pl.ds(0, 31)], ag_s.at[1])
    wait(rgr.at[pl.ds(0, 31)], rg_s)
    wait(rsel.at[pl.ds(0, 31)], gs_s.at[0])
    for cp in outs + more:
        cp.wait()


def shards(queries, key_states, values, out_grad, pattern, global_ids):
    vmem = pltpu.VMEM
    dma = pltpu.SemaphoreType.DMA
    anyspace = pl.BlockSpec(memory_space=pl.ANY)
    smem = pl.BlockSpec(memory_space=pltpu.SMEM)
    out = jax.ShapeDtypeStruct((BLK, 512), BF)
    return pl.pallas_call(
        kernel,
        out_shape=(out, out, out),
        in_specs=[smem, smem, anyspace, anyspace, anyspace, anyspace],
        out_specs=(anyspace, anyspace, anyspace),
        scratch_shapes=[
            vmem((2, BLK, 256), BF),
            vmem((2, BLK, 512), BF),
            vmem((2, BLK, 512), BF),
            vmem((2, BLK, 256), BF),
            vmem((BLK, 512), BF),
            vmem((32, 16, 128), BF),
            vmem((2, 16, 128), BF),
            vmem((2, BLK, 512), BF),
            vmem((2, BLK, 512), BF),
            vmem((32, 2, 16, 128), BF),
            vmem((2, 16, 128), BF),
            vmem((BLK, 512), BF),
            vmem((BLK, 512), BF),
            vmem((2, 2, BLK, 256), BF),
            vmem((2, 2, BLK, 256), BF),
            vmem((2, BLK, 512), F32),
            vmem((2, BLK, 512), BF),
            vmem((2, BLK, 256), BF),
            vmem((2, 384, 256), F32),
            vmem((2, 384, 256), F32),
            vmem((2, 256, 256), BF),
            dma((3,)),
            dma((3,)), dma((3,)),
            dma((2,)), dma((2,)),
            dma, dma,
            dma, dma,
            dma, dma,
            dma((2,)), dma((2,)),
            dma, dma,
            dma((2,)), dma((2,)),
            dma((2, 2)), dma((2, 2)),
            dma((3,)), dma((3,)), dma((3,)),
        ],
        name="block_attention_grads",
        compiler_params=pltpu.CompilerParams(
            collective_id=0, has_side_effects=True, vmem_limit_bytes=32 * 1024 * 1024
        ),
    )(pattern, global_ids, queries, key_states, values, out_grad)


def solution(mesh):
    placed = (
        P("ctx", "head"),
        P("ctx", "head"),
        P("ctx", "head"),
        P(("ctx", "head"), None),
        P(),
        P(),
    )
    return jax.shard_map(
        shards,
        mesh=mesh,
        in_specs=placed,
        out_specs=(P("ctx", "head"), P("ctx", "head"), P("ctx", "head")),
        check_vma=False,
    )
```

time: 1140 us -> 66.8 us (0.06)
  waiting for transfers between devices: 1060 us -> 0 us
  Pallas kernels: 0 us -> 59.6 us
  starting transfers between devices: 24.1 us -> 0 us
  local copies, waits for them, and re-layouts: 21.4 us -> 6.36 us
  between operations: 15.6 us -> 0.66 us
  other arithmetic: 14.7 us -> 0 us
    psum x2 -> x0, waiting for transfers between devices: 1050 us -> none  [the longest x1 530 us: from_root(): return lax.psum(jnp.where(mine, value, jnp.zeros_like(value)), axis)]
    pallas_call x0 -> x1, Pallas kernels: none -> 59.6 us  [shards(): pl.pallas_call(kernel, out_shape=(out, out, out), in_specs=[smem, smem, a...]
    ppermute x4 -> x0, starting transfers between devices: 15.8 us -> none  [the longest x2 10.9 us: padded(): lax.ppermute(head, axis, [((i + 1) % count, i) for i in range(count)])]
  transfers between devices with their start and end apart: 7 -> 0, of which waited for: 3 -> 0; matrix products, arithmetic and copies ran while one was open for 1% -> 0% of each run, Pallas kernels for 0% -> 0%
where the time goes in v1:
time: 66.8 us; the launch traced here: 66.6 us
  Pallas kernels  59.6 us (89%)
  local copies, waits for them, and re-layouts  6.36 us (10%)
    pallas_call x1, Pallas kernels, shards(): pl.pallas_call(kernel, out_shape=(out, out, out), in_specs=[smem, smem, a...  59.6 us
    unnamed x14, local copies, waits for them, and re-layouts  6.36 us

profile of v1, /device:TPU:1, one launch (start us, length us, event | category | flops | bytes accessed | tf_op | source)
XLA Modules:
  0.0 66.6 jit_solution(14319096718892602076)
XLA Ops:
  0.6 0.0 copy-start.4
  0.6 0.8 %copy.9.pat = s32[64,3]{1,0:T(8,128)S(1)} copy(s32[64,3]{0,1:T(4,128)} %param.10) | data formatting | bytes 1536 | tf_op args[4]
  1.4 0.0 copy-done.4
  1.4 0.0 copy-start
  1.4 0.9 %copy-done = bf16[128,512]{1,0:T(8,128)(2,1)S(1)} copy-done((bf16[128,512]{1,0:T(8,128)(2,1)S(1)}, bf16[128,512]{1,0:T(8,128)(2,1)}, u32[]{:S(2)}) %copy-start) | copy-done | bytes 131096
  2.3 0.0 copy-start.1
  2.3 0.9 %copy-done.1 = bf16[128,512]{1,0:T(8,128)(2,1)S(1)} copy-done((bf16[128,512]{1,0:T(8,128)(2,1)S(1)}, bf16[128,512]{1,0:T(8,128)(2,1)}, u32[]{:S(2)}) %copy-start.1) | copy-done | bytes 131096
  3.2 0.0 copy-start.2
  3.2 0.9 %copy-done.2 = bf16[128,512]{1,0:T(8,128)(2,1)S(1)} copy-done((bf16[128,512]{1,0:T(8,128)(2,1)S(1)}, bf16[128,512]{1,0:T(8,128)(2,1)}, u32[]{:S(2)}) %copy-start.2) | copy-done | bytes 131096
  4.1 0.0 copy-start.3
  4.1 0.9 %copy-done.3 = bf16[16,4096]{1,0:T(8,128)(2,1)S(1)} copy-done((bf16[16,4096]{1,0:T(8,128)(2,1)S(1)}, bf16[16,4096]{1,0:T(8,128)(2,1)}, u32[]{:S(2)}) %copy-start.3) | copy-done | bytes 131096
  5.0 59.6 %block_attention_grads.1 = (bf16[128,512]{1,0:T(8,128)(2,1)S(1)}, bf16[128,512]{1,0:T(8,128)(2,1)S(1)}, bf16[128,512]{1,0:T(8,128)(2,1)S(1)}) custom-call(s32[64,3]{1,0:T(8,128)S(1)} %copy.9.pat, s32[2]{0:T(128)S(1)} %copy-done.4, bf16[128,512]{1,0:T(8,128)(2,1)S(1)} %copy-done, bf16[128,512]{1,0:T(8,128)(2,1)S(1)} %copy-done.1, ...), custom_call_target="tpu_custom_call" | custom-call | tf_op jit(solution)/shard_map/block_attention_grads/pallas_call | solution.py:354
  64.6 0.7 copy.13
  65.3 0.7 copy.14
  66.0 0.7 copy.15
Async XLA Ops:
  0.6 0.8 %copy-start.4 = (s32[2]{0:T(128)S(1)}, s32[2]{0:T(128)}, u32[]{:S(2)}) copy-start(s32[2]{0:T(128)} %gid.1) | copy-start | bytes 28
  1.4 0.9 %copy-start = (bf16[128,512]{1,0:T(8,128)(2,1)S(1)}, bf16[128,512]{1,0:T(8,128)(2,1)}, u32[]{:S(2)}) copy-start(bf16[128,512]{1,0:T(8,128)(2,1)} %q_ref.1) | copy-start | bytes 393220
  2.3 0.9 %copy-start.1 = (bf16[128,512]{1,0:T(8,128)(2,1)S(1)}, bf16[128,512]{1,0:T(8,128)(2,1)}, u32[]{:S(2)}) copy-start(bf16[128,512]{1,0:T(8,128)(2,1)} %k_ref.1) | copy-start | bytes 393220
  3.2 0.9 %copy-start.2 = (bf16[128,512]{1,0:T(8,128)(2,1)S(1)}, bf16[128,512]{1,0:T(8,128)(2,1)}, u32[]{:S(2)}) copy-start(bf16[128,512]{1,0:T(8,128)(2,1)} %v_ref.1) | copy-start | bytes 393220
  4.1 0.9 %copy-start.3 = (bf16[16,4096]{1,0:T(8,128)(2,1)S(1)}, bf16[16,4096]{1,0:T(8,128)(2,1)}, u32[]{:S(2)}) copy-start(bf16[16,4096]{1,0:T(8,128)(2,1)} %g_ref.1) | copy-start | bytes 393220

commit v2 on v1

--- a/solution.py
+++ b/solution.py
@@ -19,15 +19,34 @@
 TN = (((0,), (0,)), ((), ()))
 
 
+def remote(src, dst, ss, rs, dev):
+    return pltpu.make_async_remote_copy(
+        src_ref=src, dst_ref=dst, send_sem=ss, recv_sem=rs,
+        device_id=dev, device_id_type=MESH,
+    )
+
+
+def local(src, dst, sem):
+    return pltpu.make_async_copy(src, dst, sem)
+
+
+def wait(ref, sem):
+    pltpu.make_async_copy(ref, ref, sem).wait()
+
+
+def signal(sem, dev):
+    pl.semaphore_signal(sem, inc=1, device_id=dev, device_id_type=MESH)
+
+
 def dot(a, b, dims):
     return lax.dot_general(a, b, dims, preferred_element_type=F32)
 
 
 def kernel(
-    pat, gid, q_ref, k_ref, v_ref, g_ref, dq_ref, dk_ref, dv_ref,
-    q2, kv2, kvn, do2, cand, rsel, hold, gkv, gpart, rgr, hsum, gs0, gs63,
+    pat_ref, gid_ref, q_ref, k_ref, v_ref, g_ref, all_ref,
+    pat, gid, q2, kv2, kvn, do2, cand, rsel, hold, gkv, gpart, rgr, hsum, gs0, gs63,
     nbo, nbi, own, fin, dqb, el, dpl, dsg,
-    in_sem, pair_s, pair_r, nb_s, nb_r, do_s, do_r, sel_s, sel_r, sc_s, sc_r,
+    ok_sib, ok_group, ok_plane, in_sem, pair_s, pair_r, nb_s, nb_r, do_s, do_r, sel_s, sel_r, sc_s, sc_r,
     ag_s, ag_r, rg_s, rg_r, gs_s, gs_r, gn_s, gn_r, out_l, out_s, out_r,
 ):
     me = lax.axis_index("ctx")
@@ -42,50 +61,80 @@
     mine = pl.multiple_of(core * 256, 256)
     theirs = pl.multiple_of((1 - core) * 256, 256)
 
-    def remote(src, dst, ss, rs, dev):
-        return pltpu.make_async_remote_copy(
-            src_ref=src, dst_ref=dst, send_sem=ss, recv_sem=rs,
-            device_id=dev, device_id_type=MESH,
-        )
-
-    def local(src, dst, sem):
-        return pltpu.make_async_copy(src, dst, sem)
-
-    def wait(ref, sem):
-        pltpu.make_async_copy(ref, ref, sem).wait()
-
-    def far_y(i):
-        return (y + 4 + (1 - 2 * (i % 2)) * ((i + 1) // 2)) % 8
-
-    def plane(t):
-        ty = far_y(t // 4)
-        tz = (z + 3 - t % 4) % 4
-        return ty, tz, {"ctx": (tz * 8 + ty) * 2 + core}
-
-    def group(t):
-        th = (head + 7 - t // 2) % 8
-        tc = (core + 1 - t % 2) % 2
-        return th, tc, {"ctx": chip * 2 + tc, "head": th}
+    def around(base, step, size):
+        return jnp.where(base + step >= size, base + step - size, base + step)
+
+    ys = [around(y, d, 8) for d in range(8)]
+    zs = [around(z, d, 4) for d in range(4)]
+    plane = []
+    for dy in (4, 3, 5, 2, 6, 1, 7, 0):
+        for dz in (3, 2, 1, 0):
+            if dy or dz:
+                plane.append((ys[dy], zs[dz], {"ctx": zs[dz] * 16 + ys[dy] * 2 + core}))
+    rank = z * 8 + jnp.where(y < 4, y, 11 - y)
+    chip_at = [t // 8 * 8 + (t % 8 if t % 8 < 4 else 11 - t % 8) for t in range(32)]
+
+    def ranked(t):
+        return {"ctx": chip_at[t] * 2 + core}
+
+    def headed(th, tc):
+        return {"ctx": chip * 2 + tc, "head": th}
 
     loads = [
         local(k_ref.at[:, pl.ds(mine, 256)], kv2.at[core, :, pl.ds(0, 256)], in_sem.at[0]),
         local(v_ref.at[:, pl.ds(mine, 256)], kv2.at[core, :, pl.ds(256, 256)], in_sem.at[1]),
         local(q_ref.at[:, pl.ds(mine, 256)], q2.at[core], in_sem.at[2]),
+        local(gid_ref, gid, in_sem.at[3]),
+        local(pat_ref, pat, in_sem.at[4]),
     ]
     for cp in loads:
         cp.start()
 
     bar = pltpu.get_barrier_semaphore()
 
-    @pl.loop(0, 31)
-    def _(t):
-        pl.semaphore_signal(bar, inc=1, device_id=plane(t)[2], device_id_type=MESH)
-
-    @pl.loop(0, 15)
-    def _(t):
-        pl.semaphore_signal(bar, inc=1, device_id=group(t)[2], device_id_type=MESH)
-
-    pl.semaphore_wait(bar, 46)
+    @pl.when(core == 0)
+    def _():
+        signal(bar, sib)
+
+    for t in range(1, 32):
+
+        @pl.when(t > rank)
+        def _():
+            signal(bar, ranked(t))
+
+    for th in range(1, 8):
+
+        @pl.when(th > head)
+        def _():
+            signal(bar, headed(th, 0))
+            signal(bar, headed(th, 1))
+
+    lower = rank + 2 * head + core
+
+    @pl.when(lower > 0)
+    def _():
+        pl.semaphore_wait(bar, lower)
+
+    @pl.when(core == 1)
+    def _():
+        signal(ok_sib, sib)
+
+    for t in range(31):
+
+        @pl.when(t < rank)
+        def _():
+            signal(ok_plane.at[rank], ranked(t))
+
+    for th in range(7):
+
+        @pl.when(th < head)
+        def _():
+            signal(ok_group, headed(th, 0))
+            signal(ok_group, headed(th, 1))
+
+    @pl.when(core == 0)
+    def _():
+        pl.semaphore_wait(ok_sib, 1)
 
     pairs = [
         remote(k_ref.at[:, pl.ds(theirs, 256)], kv2.at[core, :, pl.ds(0, 256)], pair_s.at[0], pair_r.at[0], sib),
@@ -102,48 +151,80 @@
     def piece(ref, tz, ty):
         return ref.at[pl.ds(pl.multiple_of(ty * 16, 16), 16), pl.ds(pl.multiple_of(tz * 128, 128), 128)]
 
-    @pl.when(chip == 31)
-    def _():
-        @pl.loop(0, 31)
-        def _(t):
-            ty, tz, dev = plane(t)
-            remote(piece(kv2.at[1], tz, ty), hold.at[1], sc_s, sc_r, dev).start()
-
-        local(piece(kv2.at[1], z, y), hold.at[1], sc_r).start()
-
+    loads[3].wait()
     g0 = gid[0]
     cand[...] = kv2[g0 % 2]
-
-    @pl.loop(0, 31)
-    def _(t):
-        ty, tz, dev = plane(t)
-        remote(piece(cand, tz, ty), rsel.at[chip], sel_s, sel_r, dev).start()
-
-    local(piece(cand, z, y), rsel.at[chip], sel_r).start()
-
     nbk = [
         remote(kv2.at[1], kvn.at[0], nb_s.at[0], nb_r.at[0], right),
         remote(kv2.at[0], kvn.at[1], nb_s.at[1], nb_r.at[1], left),
     ]
-    for cp in nbk:
-        cp.start()
+    right_chip = around(chip, 1, 32)
+    left_chip = around(chip, 31, 32)
+
+    def first(t):
+        tz, ty = chip_at[t] // 8, chip_at[t] % 8
+
+        @pl.when(chip == 31)
+        def _():
+            remote(piece(kv2.at[1], tz, ty), hold.at[1], sc_s, sc_r, ranked(t)).start()
+
+        remote(piece(cand, tz, ty), rsel.at[chip], sel_s, sel_r, ranked(t)).start()
+
+        @pl.when(right_chip == chip_at[t])
+        def _():
+            nbk[0].start()
+
+        @pl.when(left_chip == chip_at[t])
+        def _():
+            nbk[1].start()
+
+    for t in range(31):
+
+        @pl.when(t < rank)
+        def _():
+            first(t)
+
+    local(piece(cand, z, y), rsel.at[chip], sel_r).start()
+
+    @pl.when(chip == 31)
+    def _():
+        local(piece(kv2.at[1], z, y), hold.at[1], sc_r).start()
 
     rows = pl.ds(pl.multiple_of(head * 16, 16), 16)
 
-    def gcols(th, tc):
-        return pl.ds(pl.multiple_of(th * 512 + tc * 256, 256), 256)
-
-    @pl.loop(0, 15)
-    def _(t):
-        th, tc, dev = group(t)
-        remote(g_ref.at[:, gcols(th, tc)], do2.at[core, rows], do_s, do_r, dev).start()
-
-    local(g_ref.at[:, gcols(head, core)], do2.at[core, rows], do_r).start()
+    def give(th, tc):
+        cols = pl.ds(pl.multiple_of(th * 512 + tc * 256, 256), 256)
+        return remote(g_ref.at[:, cols], do2.at[core, rows], do_s, do_r, headed(th, tc))
+
+    give(head, 1 - core).start()
+    local(g_ref.at[:, pl.ds(pl.multiple_of(head * 512 + core * 256, 256), 256)], do2.at[core, rows], do_r).start()
+    for th in range(7):
+
+        @pl.when(th < head)
+        def _():
+            give(th, 0).start()
+            give(th, 1).start()
+
+    for t in range(1, 32):
+
+        @pl.when(t > rank)
+        def _():
+            pl.semaphore_wait(ok_plane.at[t], 1)
+            first(t)
+
+    @pl.when(head < 7)
+    def _():
+        pl.semaphore_wait(ok_group, 2 * (7 - head))
+
+    for th in range(1, 8):
+
+        @pl.when(th > head)
+        def _():
+            give(th, 0).start()
+            give(th, 1).start()
 
     def spread(g):
-        @pl.loop(0, 31)
-        def _(t):
-            _, _, dev = plane(t)
+        for _, _, dev in plane:
             remote(hold.at[g], piece(gkv.at[g], z, y), ag_s.at[g], ag_r.at[g], dev).start()
 
         local(hold.at[g], piece(gkv.at[g], z, y), ag_r.at[g]).start()
@@ -155,6 +236,7 @@
     spread(0)
 
     loads[2].wait()
+    loads[4].wait()
     pairs[2].wait_recv()
     nbk[0].wait_recv()
     nbk[1].wait_recv()
@@ -163,7 +245,7 @@
     def count(block, target):
         n = jnp.int32(1)
         for r in range(3):
-            n = n + jnp.where(pat[block, r] == target, 1, 0)
+            n = n + jnp.where(pat[r, block] == target, 1, 0)
         return n.astype(F32)
 
     b0, b1 = chip * 2, chip * 2 + 1
@@ -222,20 +304,21 @@
         gpart[:, :, vc] = dot(p.astype(BF), gh, NN).astype(BF).reshape(2, 128, 128)
         rowf.append((scale_l * inv, delta))
 
-        @pl.loop(0, 16)
-        def _(t):
-            ty = far_y(t // 2)
-            tz = hh + 2 * (t % 2)
-            src = gpart.at[:, pl.ds(pl.multiple_of(ty * 16, 16), 16), pl.ds(pl.multiple_of(tz * 128, 128), 128)]
-            self_piece = jnp.logical_and(ty == y, tz == z)
-
-            @pl.when(self_piece)
-            def _():
-                local(src, rgr.at[chip], rg_r).start()
-
-            @pl.when(jnp.logical_not(self_piece))
-            def _():
-                remote(src, rgr.at[chip], rg_s, rg_r, {"ctx": (tz * 8 + ty) * 2 + core}).start()
+        for dy in (4, 3, 5, 2, 6, 1, 7, 0):
+            for tz in (hh, hh + 2):
+                src = gpart.at[:, pl.ds(pl.multiple_of(ys[dy] * 16, 16), 16), pl.ds(tz * 128, 128)]
+                dev = {"ctx": tz * 16 + ys[dy] * 2 + core}
+                if dy:
+                    remote(src, rgr.at[chip], rg_s, rg_r, dev).start()
+                    continue
+
+                @pl.when(z == tz)
+                def _():
+                    local(src, rgr.at[chip], rg_r).start()
+
+                @pl.when(z != tz)
+                def _():
+                    remote(src, rgr.at[chip], rg_s, rg_r, dev).start()
 
     nbg = []
     for hh in range(2):
@@ -265,8 +348,8 @@
 
     my_cols = pl.ds(mine, 256)
     outs = [
-        remote(dqb.at[1 - core], dq_ref.at[:, my_cols], out_s.at[0], out_r.at[0], sib),
-        local(dqb.at[core], dq_ref.at[:, my_cols], out_l.at[0]),
+        remote(dqb.at[1 - core], all_ref.at[0, :, my_cols], out_s.at[0], out_r.at[0], sib),
+        local(dqb.at[core], all_ref.at[0, :, my_cols], out_l.at[0]),
     ]
     for cp in outs:
         cp.start()
@@ -277,9 +360,7 @@
         acc = acc + rgr[j].astype(F32)
     hsum[...] = acc.astype(BF)
 
-    @pl.loop(0, 31)
-    def _(t):
-        _, _, dev = plane(t)
+    for _, _, dev in plane:
         remote(hsum.at[0], piece(gs0, z, y), gs_s.at[0], gs_r.at[0], dev).start()
 
     local(hsum.at[0], piece(gs0, z, y), gs_r.at[0]).start()
@@ -312,10 +393,10 @@
 
     lo, hi = pl.ds(0, 256), pl.ds(256, 256)
     more = [
-        remote(fin.at[1 - core, :, lo], dk_ref.at[:, my_cols], out_s.at[1], out_r.at[1], sib),
-        remote(fin.at[1 - core, :, hi], dv_ref.at[:, my_cols], out_s.at[2], out_r.at[2], sib),
-        local(fin.at[core, :, lo], dk_ref.at[:, my_cols], out_l.at[1]),
-        local(fin.at[core, :, hi], dv_ref.at[:, my_cols], out_l.at[2]),
+        remote(fin.at[1 - core, :, lo], all_ref.at[1, :, my_cols], out_s.at[1], out_r.at[1], sib),
+        remote(fin.at[1 - core, :, hi], all_ref.at[2, :, my_cols], out_s.at[2], out_r.at[2], sib),
+        local(fin.at[core, :, lo], all_ref.at[1, :, my_cols], out_l.at[1]),
+        local(fin.at[core, :, hi], all_ref.at[2, :, my_cols], out_l.at[2]),
     ]
     for cp in more:
         cp.start()
@@ -348,15 +429,19 @@
 def shards(queries, key_states, values, out_grad, pattern, global_ids):
     vmem = pltpu.VMEM
     dma = pltpu.SemaphoreType.DMA
+    hbm = pl.BlockSpec(memory_space=pltpu.HBM)
     anyspace = pl.BlockSpec(memory_space=pl.ANY)
     smem = pl.BlockSpec(memory_space=pltpu.SMEM)
-    out = jax.ShapeDtypeStruct((BLK, 512), BF)
-    return pl.pallas_call(
+    out = jax.ShapeDtypeStruct((3, BLK, 512), BF)
+    operands = (pattern.T, global_ids, queries, key_states, values, out_grad)
+    grads = pl.pallas_call(
         kernel,
-        out_shape=(out, out, out),
-        in_specs=[smem, smem, anyspace, anyspace, anyspace, anyspace],
-        out_specs=(anyspace, anyspace, anyspace),
+        out_shape=out,
+        in_specs=[hbm] * 6,
+        out_specs=anyspace,
         scratch_shapes=[
+            pltpu.SMEM((3, 64), jnp.int32),
+            pltpu.SMEM((2,), jnp.int32),
             vmem((2, BLK, 256), BF),
             vmem((2, BLK, 512), BF),
             vmem((2, BLK, 512), BF),
@@ -378,7 +463,8 @@
             vmem((2, 384, 256), F32),
             vmem((2, 384, 256), F32),
             vmem((2, 256, 256), BF),
-            dma((3,)),
+            pltpu.SemaphoreType.REGULAR, pltpu.SemaphoreType.REGULAR, pltpu.SemaphoreType.REGULAR((32,)),
+            dma((5,)),
             dma((3,)), dma((3,)),
             dma((2,)), dma((2,)),
             dma, dma,
@@ -394,7 +480,8 @@
         compiler_params=pltpu.CompilerParams(
             collective_id=0, has_side_effects=True, vmem_limit_bytes=32 * 1024 * 1024
         ),
-    )(pattern, global_ids, queries, key_states, values, out_grad)
+    )(*[pltpu.with_memory_space_constraint(a, pltpu.HBM) for a in operands])
+    return grads[0], grads[1], grads[2]
 
 
 def solution(mesh):

time: 66.8 us -> 51.9 us (0.78)
  Pallas kernels: 59.6 us -> 50.3 us
  local copies, waits for them, and re-layouts: 6.36 us -> 0.75 us
    pallas_call x1, Pallas kernels: 59.6 us -> 50.3 us  [shards(): pl.pallas_call(kernel, out_shape=out, in_specs=[hbm] * 6, out_specs=anysp...]
    unnamed x14 -> x0, local copies, waits for them, and re-layouts: 6.36 us -> none
    squeeze x0 -> x1, local copies, waits for them, and re-layouts: none -> 0.75 us  [shards(): return (grads[0], grads[1], grads[2])]
where the time goes in v2:
time: 51.9 us; the launch traced here: 51.7 us
  Pallas kernels  50.3 us (97%)
  local copies, waits for them, and re-layouts  0.75 us (1%)
  between operations  0.64 us (1%)
    pallas_call x1, Pallas kernels, shards(): pl.pallas_call(kernel, out_shape=out, in_specs=[hbm] * 6, out_specs=anysp...  50.3 us

profile of v2, /device:TPU:1, one launch (start us, length us, event | category | flops | bytes accessed | tf_op | source)
XLA Modules:
  0.0 51.7 jit_solution(11479996320832305677)
XLA Ops:
  0.6 50.3 %block_attention_grads.1 = bf16[3,128,512]{2,1,0:T(8,128)(2,1)S(1)} custom-call(s32[3,64]{1,0:T(4,128)} %bitcast.7, s32[2]{0:T(128)} %gid_ref.1, bf16[128,512]{1,0:T(8,128)(2,1)} %q_ref.1, bf16[128,512]{1,0:T(8,128)(2,1)} %k_ref.1, bf16[128,512]{1,0:T(8,128)(2,1)} %v_ref.1, bf16[16,4096]{1,0:T(8,128)(2,1)} %g_ref.1), custom_call_target="tpu_custom_call" | custom-call | tf_op jit(solution)/shard_map/block_attention_grads/pallas_call | solution.py:437
  51.0 0.8 %slice_bitcast_fusion = (bf16[128,512]{1,0:T(8,128)(2,1)}, bf16[128,512]{1,0:T(8,128)(2,1)}, bf16[128,512]{1,0:T(8,128)(2,1)}) fusion(bf16[3,128,512]{2,1,0:T(8,128)(2,1)S(1)} %block_attention_grads.1), kind=kLoop, calls=%fused_computation | loop fusion | bytes 786432 | tf_op jit(solution)/shard_map/squeeze | solution.py:484

commit v3 on v2

--- a/solution.py
+++ b/solution.py
@@ -71,11 +71,11 @@
         for dz in (3, 2, 1, 0):
             if dy or dz:
                 plane.append((ys[dy], zs[dz], {"ctx": zs[dz] * 16 + ys[dy] * 2 + core}))
-    rank = z * 8 + jnp.where(y < 4, y, 11 - y)
-    chip_at = [t // 8 * 8 + (t % 8 if t % 8 < 4 else 11 - t % 8) for t in range(32)]
-
-    def ranked(t):
-        return {"ctx": chip_at[t] * 2 + core}
+    row = z * 8
+    above = row + 8
+
+    def at_chip(t):
+        return {"ctx": t * 2 + core}
 
     def headed(th, tc):
         return {"ctx": chip * 2 + tc, "head": th}
@@ -96,41 +96,33 @@
     def _():
         signal(bar, sib)
 
-    for t in range(1, 32):
-
-        @pl.when(t > rank)
-        def _():
-            signal(bar, ranked(t))
-
-    for th in range(1, 8):
-
-        @pl.when(th > head)
-        def _():
-            signal(bar, headed(th, 0))
-            signal(bar, headed(th, 1))
-
-    lower = rank + 2 * head + core
-
-    @pl.when(lower > 0)
-    def _():
-        pl.semaphore_wait(bar, lower)
+    @pl.loop(row, chip)
+    def _(t):
+        signal(bar, at_chip(t))
+
+    @pl.loop(chip + 1, 32)
+    def _(t):
+        signal(bar, at_chip(t))
+
+    @pl.loop(head + 1, 8)
+    def _(th):
+        signal(bar, headed(th, 0))
+        signal(bar, headed(th, 1))
+
+    pl.semaphore_wait(bar, row + 7 + 2 * head + core)
 
     @pl.when(core == 1)
     def _():
         signal(ok_sib, sib)
 
-    for t in range(31):
-
-        @pl.when(t < rank)
-        def _():
-            signal(ok_plane.at[rank], ranked(t))
-
-    for th in range(7):
-
-        @pl.when(th < head)
-        def _():
-            signal(ok_group, headed(th, 0))
-            signal(ok_group, headed(th, 1))
+    @pl.loop(0, row)
+    def _(t):
+        signal(ok_plane.at[chip], at_chip(t))
+
+    @pl.loop(0, head)
+    def _(th):
+        signal(ok_group, headed(th, 0))
+        signal(ok_group, headed(th, 1))
 
     @pl.when(core == 0)
     def _():
@@ -162,33 +154,20 @@
     left_chip = around(chip, 31, 32)
 
     def first(t):
-        tz, ty = chip_at[t] // 8, chip_at[t] % 8
-
-        @pl.when(chip == 31)
-        def _():
-            remote(piece(kv2.at[1], tz, ty), hold.at[1], sc_s, sc_r, ranked(t)).start()
-
-        remote(piece(cand, tz, ty), rsel.at[chip], sel_s, sel_r, ranked(t)).start()
-
-        @pl.when(right_chip == chip_at[t])
-        def _():
-            nbk[0].start()
-
-        @pl.when(left_chip == chip_at[t])
-        def _():
-            nbk[1].start()
-
-    for t in range(31):
-
-        @pl.when(t < rank)
-        def _():
-            first(t)
+        remote(piece(cand, t // 8, t % 8), rsel.at[chip], sel_s, sel_r, at_chip(t)).start()
+
+    def root(t):
+        remote(piece(kv2.at[1], t // 8, t % 8), hold.at[1], sc_s, sc_r, at_chip(t)).start()
+
+    pl.loop(0, chip)(first)
+    pl.loop(chip + 1, above)(first)
+
+    @pl.when(chip == 31)
+    def _():
+        pl.loop(0, 31)(root)
+        local(piece(kv2.at[1], z, y), hold.at[1], sc_r).start()
 
     local(piece(cand, z, y), rsel.at[chip], sel_r).start()
-
-    @pl.when(chip == 31)
-    def _():
-        local(piece(kv2.at[1], z, y), hold.at[1], sc_r).start()
 
     rows = pl.ds(pl.multiple_of(head * 16, 16), 16)
 
@@ -198,30 +177,22 @@
 
     give(head, 1 - core).start()
     local(g_ref.at[:, pl.ds(pl.multiple_of(head * 512 + core * 256, 256), 256)], do2.at[core, rows], do_r).start()
-    for th in range(7):
-
-        @pl.when(th < head)
-        def _():
-            give(th, 0).start()
-            give(th, 1).start()
-
-    for t in range(1, 32):
-
-        @pl.when(t > rank)
-        def _():
-            pl.semaphore_wait(ok_plane.at[t], 1)
-            first(t)
-
-    @pl.when(head < 7)
-    def _():
-        pl.semaphore_wait(ok_group, 2 * (7 - head))
-
-    for th in range(1, 8):
-
-        @pl.when(th > head)
-        def _():
-            give(th, 0).start()
-            give(th, 1).start()
+
+    @pl.loop(0, head)
+    def _(th):
+        give(th, 0).start()
+        give(th, 1).start()
+
+    def rest(t):
+        pl.semaphore_wait(ok_plane.at[t], 1)
+        first(t)
+
+    split = jnp.maximum(above, 24)
+    pl.loop(above, split)(rest)
+    pl.loop(split, 32)(rest)
+    for cp in nbk:
+        cp.start()
+
 
     def spread(g):
         for _, _, dev in plane:
@@ -234,6 +205,15 @@
     wait(rsel, sel_r)
     hold[0] = rsel[g0 // 2]
     spread(0)
+
+    @pl.when(head < 7)
+    def _():
+        pl.semaphore_wait(ok_group, 2 * (7 - head))
+
+    @pl.loop(head + 1, 8)
+    def _(th):
+        give(th, 0).start()
+        give(th, 1).start()
 
     loads[2].wait()
     loads[4].wait()
@@ -285,6 +265,23 @@
     wait(gkv.at[1], ag_r.at[1])
     wait(gkv.at[0], ag_r.at[0])
     rowf = []
+
+    def reduce_to(g, tz, dy):
+        src = gpart.at[g, pl.ds(pl.multiple_of(ys[dy] * 16, 16), 16), pl.ds(tz * 128, 128)]
+        dst = rgr.at[g, chip]
+        push = remote(src, dst, rg_s.at[g], rg_r.at[g], {"ctx": tz * 16 + ys[dy] * 2 + core})
+        if dy:
+            push.start()
+            return
+
+        @pl.when(z == tz)
+        def _():
+            local(src, dst, rg_r.at[g]).start()
+
+        @pl.when(z != tz)
+        def _():
+            push.start()
+
     for hh in range(2):
         kc, vc = cols(hh)
         top_l, total_l, dsum_l = stats[hh]
@@ -306,19 +303,11 @@
 
         for dy in (4, 3, 5, 2, 6, 1, 7, 0):
             for tz in (hh, hh + 2):
-                src = gpart.at[:, pl.ds(pl.multiple_of(ys[dy] * 16, 16), 16), pl.ds(tz * 128, 128)]
-                dev = {"ctx": tz * 16 + ys[dy] * 2 + core}
-                if dy:
-                    remote(src, rgr.at[chip], rg_s, rg_r, dev).start()
-                    continue
-
-                @pl.when(z == tz)
-                def _():
-                    local(src, rgr.at[chip], rg_r).start()
-
-                @pl.when(z != tz)
-                def _():
-                    remote(src, rgr.at[chip], rg_s, rg_r, dev).start()
+                reduce_to(0, tz, dy)
+
+    for dy in (4, 3, 5, 2, 6, 1, 7, 0):
+        for tz in range(4):
+            reduce_to(1, tz, dy)
 
     nbg = []
     for hh in range(2):
@@ -334,9 +323,12 @@
         nbo[1, hh, :, 0:128] = dot(ds0[:, 128:], qh[128:], NN).astype(BF)
         nbo[1, hh, :, 128:256] = dot(p0[:, 128:], gh[128:], NN).astype(BF)
         for side, dev in ((0, left), (1, right)):
-            cp = remote(nbo.at[side, hh], nbi.at[1 - side, hh], gn_s.at[side, hh], gn_r.at[1 - side, hh], dev)
-            cp.start()
-            nbg.append(cp)
+            nbg.append(remote(nbo.at[side, hh], nbi.at[1 - side, hh], gn_s.at[side, hh], gn_r.at[1 - side, hh], dev))
+
+        @pl.when(chip == 31)
+        def _():
+            nbg[-1].start()
+
         p1 = el[hh, 128:384] * rf
         ds1 = (p1 * (dpl[hh, 128:384] - delta) * SCALE).astype(BF)
         own[:, :, kc] = dot(ds1, qh, NN).reshape(2, 128, 128)
@@ -354,24 +346,32 @@
     for cp in outs:
         cp.start()
 
-    wait(rgr, rg_r)
-    acc = rgr[0].astype(F32)
-    for j in range(1, 32):
-        acc = acc + rgr[j].astype(F32)
-    hsum[...] = acc.astype(BF)
-
-    for _, _, dev in plane:
-        remote(hsum.at[0], piece(gs0, z, y), gs_s.at[0], gs_r.at[0], dev).start()
+    def total(g):
+        wait(rgr.at[g], rg_r.at[g])
+        acc = rgr[g, 0].astype(F32)
+        for j in range(1, 32):
+            acc = acc + rgr[g, j].astype(F32)
+        hsum[g] = acc.astype(BF)
+
+    total(0)
+    for tz in range(4):
+        for dy in (4, 3, 5, 2, 6, 1, 7):
+            dev = {"ctx": tz * 16 + ys[dy] * 2 + core}
+            remote(hsum.at[0], piece(gs0, z, y), gs_s.at[0], gs_r.at[0], dev).start()
+
+        @pl.when(z != tz)
+        def _():
+            dev = {"ctx": tz * 16 + y * 2 + core}
+            remote(hsum.at[0], piece(gs0, z, y), gs_s.at[0], gs_r.at[0], dev).start()
 
     local(hsum.at[0], piece(gs0, z, y), gs_r.at[0]).start()
-
-    @pl.when(chip == 31)
-    def _():
-        local(hsum.at[1], piece(gs63, z, y), gs_r.at[1]).start()
+    nbg[0].start()
+    nbg[2].start()
 
     @pl.when(chip != 31)
     def _():
-        remote(hsum.at[1], piece(gs63, z, y), gs_s.at[1], gs_r.at[1], {"ctx": 62 + core}).start()
+        nbg[1].start()
+        nbg[3].start()
 
     for cp in nbg:
         cp.wait_recv()
@@ -380,17 +380,7 @@
             kc, vc = cols(hh)
             own[b, :, kc] += nbi[b, hh, :, 0:128].astype(F32)
             own[b, :, vc] += nbi[b, hh, :, 128:256].astype(F32)
-
-    @pl.when(chip == 31)
-    def _():
-        wait(gs63, gs_r.at[1])
-        own[1] += gs63[...].astype(F32)
-
     wait(gs0, gs_r.at[0])
-    for b in range(2):
-        pick = jnp.where(g0 == b0 + b, 1.0, 0.0).astype(F32)
-        fin[b] = (own[b] + gs0[...].astype(F32) * pick).astype(BF)
-
     lo, hi = pl.ds(0, 256), pl.ds(256, 256)
     more = [
         remote(fin.at[1 - core, :, lo], all_ref.at[1, :, my_cols], out_s.at[1], out_r.at[1], sib),
@@ -398,8 +388,30 @@
         local(fin.at[core, :, lo], all_ref.at[1, :, my_cols], out_l.at[1]),
         local(fin.at[core, :, hi], all_ref.at[2, :, my_cols], out_l.at[2]),
     ]
-    for cp in more:
-        cp.start()
+
+    def finish():
+        for b in range(2):
+            pick = jnp.where(g0 == b0 + b, 1.0, 0.0).astype(F32)
+            fin[b] = (own[b] + gs0[...].astype(F32) * pick).astype(BF)
+        for cp in more:
+            cp.start()
+
+    @pl.when(chip != 31)
+    def _():
+        finish()
+
+    total(1)
+
+    @pl.when(chip == 31)
+    def _():
+        local(hsum.at[1], piece(gs63, z, y), gs_r.at[1]).start()
+        wait(gs63, gs_r.at[1])
+        own[1] += gs63[...].astype(F32)
+        finish()
+
+    @pl.when(chip != 31)
+    def _():
+        remote(hsum.at[1], piece(gs63, z, y), gs_s.at[1], gs_r.at[1], {"ctx": 62 + core}).start()
 
     for cp in pairs:
         cp.wait_send()
@@ -420,7 +432,8 @@
     wait(rsel.at[pl.ds(0, 30)], do_s)
     wait(rsel.at[pl.ds(0, 31)], ag_s.at[0])
     wait(rsel.at[pl.ds(0, 31)], ag_s.at[1])
-    wait(rgr.at[pl.ds(0, 31)], rg_s)
+    wait(rsel.at[pl.ds(0, 31)], rg_s.at[0])
+    wait(rsel.at[pl.ds(0, 31)], rg_s.at[1])
     wait(rsel.at[pl.ds(0, 31)], gs_s.at[0])
     for cp in outs + more:
         cp.wait()
@@ -451,7 +464,7 @@
             vmem((2, 16, 128), BF),
             vmem((2, BLK, 512), BF),
             vmem((2, BLK, 512), BF),
-            vmem((32, 2, 16, 128), BF),
+            vmem((2, 32, 16, 128), BF),
             vmem((2, 16, 128), BF),
             vmem((BLK, 512), BF),
             vmem((BLK, 512), BF),
@@ -471,7 +484,7 @@
             dma, dma,
             dma, dma,
             dma((2,)), dma((2,)),
-            dma, dma,
+            dma((2,)), dma((2,)),
             dma((2,)), dma((2,)),
             dma((2, 2)), dma((2, 2)),
             dma((3,)), dma((3,)), dma((3,)),

time: 51.9 us -> 48.5 us (0.934)
  Pallas kernels: 50.3 us -> 46.9 us
    pallas_call x1, Pallas kernels: 50.3 us -> 46.9 us  [shards(): pl.pallas_call(kernel, out_shape=out, in_specs=[hbm] * 6, out_specs=anysp...]
where the time goes in v3:
time: 48.5 us; the launch traced here: 48.3 us
  Pallas kernels  46.9 us (97%)
  local copies, waits for them, and re-layouts  0.75 us (2%)
  between operations  0.64 us (1%)
    pallas_call x1, Pallas kernels, shards(): pl.pallas_call(kernel, out_shape=out, in_specs=[hbm] * 6, out_specs=anysp...  46.9 us

profile of v3, /device:TPU:1, one launch (start us, length us, event | category | flops | bytes accessed | tf_op | source)
XLA Modules:
  0.0 48.3 jit_solution(8943608861407056902)
XLA Ops:
  0.6 46.9 %block_attention_grads.1 = bf16[3,128,512]{2,1,0:T(8,128)(2,1)S(1)} custom-call(s32[3,64]{1,0:T(4,128)} %bitcast.7, s32[2]{0:T(128)} %gid_ref.1, bf16[128,512]{1,0:T(8,128)(2,1)} %q_ref.1, bf16[128,512]{1,0:T(8,128)(2,1)} %k_ref.1, bf16[128,512]{1,0:T(8,128)(2,1)} %v_ref.1, bf16[16,4096]{1,0:T(8,128)(2,1)} %g_ref.1), custom_call_target="tpu_custom_call" | custom-call | tf_op jit(solution)/shard_map/block_attention_grads/pallas_call | solution.py:450
  47.6 0.8 %slice_bitcast_fusion = (bf16[128,512]{1,0:T(8,128)(2,1)}, bf16[128,512]{1,0:T(8,128)(2,1)}, bf16[128,512]{1,0:T(8,128)(2,1)}) fusion(bf16[3,128,512]{2,1,0:T(8,128)(2,1)S(1)} %block_attention_grads.1), kind=kLoop, calls=%fused_computation | loop fusion | bytes 786432 | tf_op jit(solution)/shard_map/squeeze | solution.py:497

commit v4 on v3

--- a/solution.py
+++ b/solution.py
@@ -80,6 +80,25 @@
     def headed(th, tc):
         return {"ctx": chip * 2 + tc, "head": th}
 
+    bar = pltpu.get_barrier_semaphore()
+
+    @pl.when(core == 0)
+    def _():
+        signal(bar, sib)
+
+    @pl.loop(row, chip)
+    def _(t):
+        signal(bar, at_chip(t))
+
+    @pl.loop(chip + 1, 32)
+    def _(t):
+        signal(bar, at_chip(t))
+
+    @pl.loop(head + 1, 8)
+    def _(th):
+        signal(bar, headed(th, 0))
+        signal(bar, headed(th, 1))
+
     loads = [
         local(k_ref.at[:, pl.ds(mine, 256)], kv2.at[core, :, pl.ds(0, 256)], in_sem.at[0]),
         local(v_ref.at[:, pl.ds(mine, 256)], kv2.at[core, :, pl.ds(256, 256)], in_sem.at[1]),
@@ -89,25 +108,6 @@
     ]
     for cp in loads:
         cp.start()
-
-    bar = pltpu.get_barrier_semaphore()
-
-    @pl.when(core == 0)
-    def _():
-        signal(bar, sib)
-
-    @pl.loop(row, chip)
-    def _(t):
-        signal(bar, at_chip(t))
-
-    @pl.loop(chip + 1, 32)
-    def _(t):
-        signal(bar, at_chip(t))
-
-    @pl.loop(head + 1, 8)
-    def _(th):
-        signal(bar, headed(th, 0))
-        signal(bar, headed(th, 1))
 
     pl.semaphore_wait(bar, row + 7 + 2 * head + core)
 
@@ -343,9 +343,6 @@
         remote(dqb.at[1 - core], all_ref.at[0, :, my_cols], out_s.at[0], out_r.at[0], sib),
         local(dqb.at[core], all_ref.at[0, :, my_cols], out_l.at[0]),
     ]
-    for cp in outs:
-        cp.start()
-
     def total(g):
         wait(rgr.at[g], rg_r.at[g])
         acc = rgr[g, 0].astype(F32)
@@ -365,6 +362,8 @@
             remote(hsum.at[0], piece(gs0, z, y), gs_s.at[0], gs_r.at[0], dev).start()
 
     local(hsum.at[0], piece(gs0, z, y), gs_r.at[0]).start()
+    for cp in outs:
+        cp.start()
     nbg[0].start()
     nbg[2].start()
 
@@ -380,6 +379,12 @@
             kc, vc = cols(hh)
             own[b, :, kc] += nbi[b, hh, :, 0:128].astype(F32)
             own[b, :, vc] += nbi[b, hh, :, 128:256].astype(F32)
+    total(1)
+
+    @pl.when(chip != 31)
+    def _():
+        remote(hsum.at[1], piece(gs63, z, y), gs_s.at[1], gs_r.at[1], {"ctx": 62 + core}).start()
+
     wait(gs0, gs_r.at[0])
     lo, hi = pl.ds(0, 256), pl.ds(256, 256)
     more = [
@@ -390,17 +395,15 @@
     ]
 
     def finish():
-        for b in range(2):
+        for b, copies in ((1 - core, more[:2]), (core, more[2:])):
             pick = jnp.where(g0 == b0 + b, 1.0, 0.0).astype(F32)
             fin[b] = (own[b] + gs0[...].astype(F32) * pick).astype(BF)
-        for cp in more:
-            cp.start()
+            for cp in copies:
+                cp.start()
 
     @pl.when(chip != 31)
     def _():
         finish()
-
-    total(1)
 
     @pl.when(chip == 31)
     def _():
@@ -408,10 +411,6 @@
         wait(gs63, gs_r.at[1])
         own[1] += gs63[...].astype(F32)
         finish()
-
-    @pl.when(chip != 31)
-    def _():
-        remote(hsum.at[1], piece(gs63, z, y), gs_s.at[1], gs_r.at[1], {"ctx": 62 + core}).start()
 
     for cp in pairs:
         cp.wait_send()

time: 48.5 us -> 48.6 us (level)
  no operation moved by 1% of the time
where the time goes in v4:
time: 48.6 us; the launch traced here: 48.4 us
  Pallas kernels  47 us (97%)
  local copies, waits for them, and re-layouts  0.75 us (2%)
  between operations  0.64 us (1%)
    pallas_call x1, Pallas kernels, shards(): pl.pallas_call(kernel, out_shape=out, in_specs=[hbm] * 6, out_specs=anysp...  47 us

profile of v4, /device:TPU:1, one launch (start us, length us, event | category | flops | bytes accessed | tf_op | source)
XLA Modules:
  0.0 48.4 jit_solution(2654869094711005623)
XLA Ops:
  0.6 47.0 %block_attention_grads.1 = bf16[3,128,512]{2,1,0:T(8,128)(2,1)S(1)} custom-call(s32[3,64]{1,0:T(4,128)} %bitcast.7, s32[2]{0:T(128)} %gid_ref.1, bf16[128,512]{1,0:T(8,128)(2,1)} %q_ref.1, bf16[128,512]{1,0:T(8,128)(2,1)} %k_ref.1, bf16[128,512]{1,0:T(8,128)(2,1)} %v_ref.1, bf16[16,4096]{1,0:T(8,128)(2,1)} %g_ref.1), custom_call_target="tpu_custom_call" | custom-call | tf_op jit(solution)/shard_map/block_attention_grads/pallas_call | solution.py:449
  47.7 0.8 %slice_bitcast_fusion = (bf16[128,512]{1,0:T(8,128)(2,1)}, bf16[128,512]{1,0:T(8,128)(2,1)}, bf16[128,512]{1,0:T(8,128)(2,1)}) fusion(bf16[3,128,512]{2,1,0:T(8,128)(2,1)S(1)} %block_attention_grads.1), kind=kLoop, calls=%fused_computation | loop fusion | bytes 786432 | tf_op jit(solution)/shard_map/squeeze | solution.py:496
